TPU v7x, 32 devices: a whole 2x2x4 slice. The times are simulated.
32 devices in a mesh: lev: 2 (over x), gx: 8 (over z, y), gy: 2 (over core).
Axes of the slice: x: 2, y: 2, z: 4, core: 2. Of those that a mesh axis runs over, the one named last changes fastest.
Arguments:
- increments: float32 [1, 2, 80, 128, 256], P(None, None, 'lev', 'gx', 'gy'), may hold values from -6 to 6
- vert_corr: float32 [2, 80, 80], replicated, may hold values from -0.025 to 1, as said below
- kappa: float32 [2, 128, 256], P(None, 'gx', 'gy'), may hold values from 0.03 to 0.24
- sea_mask: int32 [80, 128, 256], P('lev', 'gx', 'gy'), may hold values 0 or 1
- level_count: int32 [128, 256], P('gx', 'gy'), may hold values from 10 to 75
Outputs:
- covaried: float32 [1, 2, 80, 128, 256], P(None, None, 'lev', 'gx', 'gy')
Inputs may be any that keep to these rules, and one draw needn't show every extreme that they name: vert_corr has ones on the diagonal, and each row's other entries together have magnitude below one.
All inputs are finite; a program needn't handle non-finite values. No bound on the sum of `sea_mask` on one device may be relied on, other than what follows from the above.
Results may differ from a plain program's by a relative error of at most 0.00021.
Values sent between devices are 32-bit elements; how exact they have to be, the bound alone decides.
A program may use at most 64 MiB of HBM per device.

v0:
```python
import jax
import jax.numpy as jnp
from jax import lax
from jax.experimental import pallas as pl
from jax.experimental.pallas import tpu as pltpu
from jax.sharding import PartitionSpec as P

PASSES = 10


def from_behind(block, axis, distance):
    devices = range(lax.axis_size(axis))
    route = [((i - distance) % len(devices), i) for i in devices]
    return lax.ppermute(block, axis, route)


def shifted(block, axis, distance):
    devices = range(lax.axis_size(axis))
    route = [(i - distance, i) for i in devices if i - distance in devices]
    return lax.ppermute(block, axis, route)


def padded(cells, sides, width):
    for axis, dim in sides:
        count = lax.axis_size(axis)
        head = lax.slice_in_dim(cells, 0, width, axis=dim)
        tail = lax.slice_in_dim(cells, cells.shape[dim] - width, cells.shape[dim], axis=dim)
        cells = jnp.concatenate(
            [
                lax.ppermute(tail, axis, [(i, (i + 1) % count) for i in range(count)]),
                cells,
                lax.ppermute(head, axis, [((i + 1) % count, i) for i in range(count)]),
            ],
            axis=dim,
        )
    return cells


def relax(extended, east_ext, north_ext, wet_center):
    center = extended[..., 1:-1, 1:-1]
    flux = east_ext[1:-1, 1:-1] * (extended[..., 2:, 1:-1] - center)
    flux = flux + east_ext[:-2, 1:-1] * (extended[..., :-2, 1:-1] - center)
    flux = flux + north_ext[1:-1, 1:-1] * (extended[..., 1:-1, 2:] - center)
    flux = flux + north_ext[1:-1, :-2] * (extended[..., 1:-1, :-2] - center)
    return wet_center * (center + flux)


def per_device(increments, vert_corr, kappa, sea_mask, level_count):
    lev_dev = sea_mask.shape[0]
    cells_x = sea_mask.shape[1]
    cells_y = sea_mask.shape[2]
    lev_first = lax.axis_index("lev") * lev_dev
    levels = lev_first + jnp.arange(lev_dev, dtype=jnp.int32)
    wet = sea_mask * (levels[:, None, None] < level_count[None]).astype(jnp.int32)
    wet_float = wet.astype(jnp.float32)
    masked = increments * wet_float
    own_rows = lax.dynamic_slice_in_dim(vert_corr, lev_first, lev_dev, 1)
    correlated = jnp.einsum(
        "toh,dthxy->dtoxy",
        own_rows,
        lax.all_gather(masked, "lev", axis=2, tiled=True),
        precision=lax.Precision.HIGHEST,
    )
    field = correlated * wet_float
    total_y = cells_y * lax.axis_size("gy")
    local_rows = lax.axis_index("gy") * cells_y + jnp.arange(cells_y, dtype=jnp.int32)
    open_local = (local_rows != total_y - 1).astype(jnp.float32)
    east_local = kappa[0]
    north_local = kappa[1] * open_local[None, :]
    east_low = from_behind(east_local[-1:, :], "gx", 1)
    north_low = shifted(north_local[:, -1:], "gy", 1)
    zero_row = jnp.zeros((1, cells_y), jnp.float32)
    zero_col = jnp.zeros((cells_x, 1), jnp.float32)
    east_ext = jnp.pad(jnp.concatenate([east_low, east_local, zero_row], axis=0), ((0, 0), (1, 1)))
    north_ext = jnp.pad(
        jnp.concatenate([north_low, north_local, zero_col], axis=1), ((1, 1), (0, 0))
    )

    def one_pass(step, current):
        extended = padded(current, (("gx", 3), ("gy", 4)), 1)
        return relax(extended, east_ext, north_ext, wet_float)

    field = lax.fori_loop(0, PASSES, one_pass, field)
    return field


TILE = 8
LANES = 128
WIDTH = 5
MESH = pl.DeviceIdType.MESH


def remote(src, dst, send_sem, recv_sem, device):
    return pltpu.make_async_remote_copy(
        src_ref=src,
        dst_ref=dst,
        send_sem=send_sem,
        recv_sem=recv_sem,
        device_id=device,
        device_id_type=MESH,
    )


def kernel(
    masked_ref, wet_ref, corr_ref, kappa_ref, out_ref,
    geo, own, other, field, halo, east, north, south,
    own_sems, same_sems, cross_sems, geo_sems, halo_sems, out_sems,
):
    lev, gx, gy = lax.axis_index("lev"), lax.axis_index("gx"), lax.axis_index("gy")
    count = lax.axis_size("gx")
    cells = masked_ref.shape[1]
    levels = masked_ref.shape[2]
    lanes = masked_ref.shape[3]
    tiles = levels // TILE
    width = WIDTH
    rows = cells + 2 * width
    rounds = PASSES // width
    east_dev = {"gx": lax.rem(gx + 1, count)}
    west_dev = {"gx": lax.rem(gx + count - 1, count)}
    mate = {"gy": 1 - gy}
    pair = {"lev": 1 - lev}
    cross = {"lev": 1 - lev, "gy": 1 - gy}

    barrier = pltpu.get_barrier_semaphore()
    everyone = (east_dev, west_dev, mate, pair, cross)
    for device in everyone:
        pl.semaphore_signal(barrier, inc=1, device_id=device, device_id_type=MESH)
    columns = gy * lanes + lax.broadcasted_iota(jnp.int32, (1, lanes), 1)
    is_open = (columns != lanes * lax.axis_size("gy") - 1).astype(jnp.float32)
    geo[gy, width:width + cells, 0:levels] = wet_ref[...]
    for x in range(cells):
        geo[gy, width + x, levels:levels + 1] = kappa_ref[0, x:x + 1]
        geo[gy, width + x, levels + 1:levels + 2] = kappa_ref[1, x:x + 1] * is_open
        geo[gy, width + x, levels + 2:] = jnp.zeros((TILE - 2, lanes), jnp.float32)
    pl.semaphore_wait(barrier, len(everyone))

    starts = ((0, width), (cells - width, width), (width, cells - 2 * width))
    own_copies, same_copies, cross_copies = [], [], []
    for q, (start, size) in enumerate(starts):
        span = pl.ds(start, size)
        own_copies.append(remote(
            masked_ref.at[1 - gy, span], own.at[span], own_sems.at[0, q], own_sems.at[1, q], mate))
        same_copies.append(remote(
            masked_ref.at[gy, span], other.at[gy, span],
            same_sems.at[0, q], same_sems.at[1, q], pair))
        cross_copies.append(remote(
            masked_ref.at[1 - gy, span], other.at[gy, span],
            cross_sems.at[0, q], cross_sems.at[1, q], cross))
    geo_copies = [
        remote(geo.at[gy, pl.ds(width, cells)], geo.at[gy, pl.ds(width, cells)], geo_sems.at[0, 0], geo_sems.at[1, 0], mate),
        remote(geo.at[gy, pl.ds(cells, width)],
               geo.at[gy, pl.ds(0, width)],
               geo_sems.at[0, 1], geo_sems.at[1, 1], east_dev),
        remote(geo.at[gy, pl.ds(width, width)],
               geo.at[gy, pl.ds(width + cells, width)],
               geo_sems.at[0, 2], geo_sems.at[1, 2], west_dev),
    ]
    for q in range(len(starts)):
        same_copies[q].start()
        cross_copies[q].start()
        if q == 0:
            for copy in geo_copies[1:]:
                copy.start()
            geo_copies[0].start()
        own_copies[q].start()

    mine = corr_ref[gy, pl.ds(pl.multiple_of(lev * levels, TILE), levels), :]
    swapped = jnp.concatenate([mine[:, levels:], mine[:, :levels]], axis=1)
    corr = jnp.where(lev == 0, mine, swapped)
    high = corr.astype(jnp.bfloat16)
    low = (corr - high.astype(jnp.float32)).astype(jnp.bfloat16)
    weights = jnp.concatenate([high, high, low], axis=1)

    def halo_copies(r, k):
        return (
            remote(field.at[k, pl.ds(width, width)], halo.at[r, 1, k],
                   halo_sems.at[0, r, 0, k], halo_sems.at[1, r, 0, k], west_dev),
            remote(field.at[k, pl.ds(cells, width)], halo.at[r, 0, k],
                   halo_sems.at[0, r, 1, k], halo_sems.at[1, r, 1, k], east_dev),
        )

    def vertical(x):
        mine = masked_ref[gy, x]
        theirs = own[x]
        first = jnp.where(gy == 0, mine, theirs)
        second = jnp.where(gy == 0, theirs, mine)
        near = jnp.concatenate([first, second], axis=1)
        far = jnp.concatenate([other[0, x], other[1, x]], axis=1)
        both = jnp.concatenate([near, far], axis=0)
        top = both.astype(jnp.bfloat16)
        rest = (both - top.astype(jnp.float32)).astype(jnp.bfloat16)
        stack = jnp.concatenate([top, rest, top], axis=0)
        result = jnp.dot(weights, stack, preferred_element_type=jnp.float32)
        for half in range(2):
            for k in range(tiles):
                value = result[k * TILE:(k + 1) * TILE, half * LANES:(half + 1) * LANES]
                wet = geo[half, width + x, k * TILE:(k + 1) * TILE]
                field[k, width + x, half] = value * wet

    pending = [halo_copies(0, k) for k in range(tiles)]
    forward = []
    geo_copies[0].wait()
    for q, (start, size) in enumerate(starts):
        own_copies[q].wait()
        same_copies[q].wait()
        cross_copies[q].wait()
        for x in range(start, start + size):
            vertical(x)
        if q < 2:
            for k in range(tiles):
                pending[k][q].start()
        if q == 1:
            for side, place in ((1, 0), (2, width + cells)):
                geo_copies[side].wait()
                edge = geo.at[gy, pl.ds(place, width)]
                forward.append(remote(
                    edge, edge, geo_sems.at[0, 2 + side], geo_sems.at[1, 2 + side], mate))
                forward[-1].start()
    for copy in forward:
        copy.wait()
    for half in range(2):
        for row in range(rows):
            east[row, half] = jnp.broadcast_to(geo[half, row, levels:levels + 1], (TILE, LANES))
            north[row, half] = jnp.broadcast_to(geo[half, row, levels + 1:levels + 2], (TILE, LANES))

    lane = lax.broadcasted_iota(jnp.int32, (TILE, LANES), 1)
    at_end = lane == LANES - 1
    at_start = lane == 0
    for row in range(rows):
        moved = [pltpu.roll(north[row, h], 1, 1) for h in range(2)]
        south[row, 0] = jnp.where(at_start, moved[1], moved[0])
        south[row, 1] = jnp.where(at_start, moved[0], moved[1])

    def relax_tile(r, k):
        for step in range(width):
            def row_of(row):
                if step == 0 and row < width:
                    return halo[r, 0, k, row, 0], halo[r, 0, k, row, 1]
                if step == 0 and row >= width + cells:
                    at = row - width - cells
                    return halo[r, 1, k, at, 0], halo[r, 1, k, at, 1]
                return field[k, row, 0], field[k, row, 1]

            first, last = step + 1, rows - 2 - step
            before, here = row_of(first - 1), row_of(first)
            flux = [east[first - 1, h] * (here[h] - before[h]) for h in range(2)]
            for row in range(first, last + 1):
                after = row_of(row + 1)
                turned = [pltpu.roll(here[h], LANES - 1, 1) for h in range(2)]
                up = [jnp.where(at_end, turned[1], turned[0]), turned[1]]
                back = [pltpu.roll(here[h], 1, 1) for h in range(2)]
                below = [back[0], jnp.where(at_start, back[0], back[1])]
                rise = [north[row, h] * (up[h] - here[h]) for h in range(2)]
                down = [south[row, h] * (here[h] - below[h]) for h in range(2)]
                ahead = [east[row, h] * (after[h] - here[h]) for h in range(2)]
                for h in range(2):
                    wet = geo[h, row, k * TILE:(k + 1) * TILE]
                    total = here[h] + ((ahead[h] - flux[h]) + (rise[h] - down[h]))
                    field[k, row, h] = wet * total
                here, flux = after, ahead

    out_copies = []
    for r in range(rounds):
        later = []
        for k in range(tiles):
            for copy in pending[k]:
                copy.wait()
            relax_tile(r, k)
            if r < rounds - 1:
                later.append(halo_copies(r + 1, k))
                for copy in later[-1]:
                    copy.start()
            else:
                out_copies.append(remote(
                    field.at[k, pl.ds(width, cells), 1 - gy], out_ref.at[gy, k],
                    out_sems.at[0, k], out_sems.at[1, k], mate))
                out_copies[-1].start()
                out_ref[gy, k] = field[k, width:width + cells, gy]
        pending = later
    for copy in out_copies:
        copy.wait()


def fused(increments, vert_corr, kappa, sea_mask, level_count):
    levels, cells, lanes = sea_mask.shape
    tiles = levels // TILE
    width = WIDTH
    rows = cells + 2 * width
    rounds = PASSES // width
    lev = lax.axis_index("lev")
    numbers = lev * levels + jnp.arange(levels, dtype=jnp.int32)
    turned = jnp.swapaxes(sea_mask, 0, 1)
    wet = (turned * (numbers[None, :, None] < level_count[:, None, :]).astype(jnp.int32)).astype(jnp.float32)
    masked = jnp.swapaxes(increments[0], 1, 2) * wet[None]
    vmem = pl.BlockSpec(memory_space=pltpu.VMEM)
    f32 = jnp.float32
    dma = pltpu.SemaphoreType.DMA
    result = pl.pallas_call(
        kernel,
        out_shape=jax.ShapeDtypeStruct((2, tiles, cells, TILE, lanes), f32),
        in_specs=[vmem] * 4,
        out_specs=vmem,
        scratch_shapes=[
            pltpu.VMEM((2, rows, levels + TILE, lanes), f32),
            pltpu.VMEM((cells, levels, lanes), f32),
            pltpu.VMEM((2, cells, levels, lanes), f32),
            pltpu.VMEM((tiles, rows, 2, TILE, lanes), f32),
            pltpu.VMEM((rounds, 2, tiles, width, 2, TILE, lanes), f32),
            pltpu.VMEM((rows, 2, TILE, lanes), f32),
            pltpu.VMEM((rows, 2, TILE, lanes), f32),
            pltpu.VMEM((rows, 2, TILE, lanes), f32),
            dma((2, 3)),
            dma((2, 3)),
            dma((2, 3)),
            dma((2, 5)),
            dma((2, rounds, 2, tiles)),
            dma((2, tiles)),
        ],
        compiler_params=pltpu.CompilerParams(
            collective_id=0, has_side_effects=True, vmem_limit_bytes=32 * 1024 * 1024
        ),
        cost_estimate=pl.CostEstimate(flops=60_000_000, bytes_accessed=4_000_000, transcendentals=0),
    )(masked, wet, vert_corr, kappa)
    return result.transpose(0, 1, 3, 2, 4).reshape(increments.shape)


def fits(mesh):
    shape = mesh.shape
    return shape["lev"] == 2 and shape["gy"] == 2 and shape["gx"] > 2


def solution(mesh):
    in_specs = (
        P(None, None, "lev", "gx", "gy"),
        P(),
        P(None, "gx", "gy"),
        P("lev", "gx", "gy"),
        P("gx", "gy"),
    )
    out_specs = P(None, None, "lev", "gx", "gy")
    return jax.shard_map(
        fused if fits(mesh) else per_device, mesh=mesh, in_specs=in_specs, out_specs=out_specs, check_vma=False
    )
```

profile of v0, /device:TPU:0, one launch (start us, length us, event | category | flops | bytes accessed | tf_op | source)
XLA Modules:
  0.0 37.9 jit_solution(978141272046051)
XLA Ops:
  0.0 0.0 copy-start.3
  0.0 0.0 copy-start.2
  0.0 0.7 %copy-done.3 = s32[16,128]{1,0:T(8,128)S(1)} copy-done((s32[16,128]{1,0:T(8,128)S(1)}, s32[16,128]{1,0:T(8,128)}, u32[]{:S(2)}) %copy-start.3) | copy-done | bytes 8216
  0.7 1.1 %fusion.wet_ref = f32[16,40,128]{2,1,0:T(8,128)S(1)} fusion(s32[40,16,128]{2,1,0:T(8,128)} %param.8, s32[16,128]{1,0:T(8,128)S(1)} %copy-done.3, s32[40]{0:T(128)S(1)} %iota_add_fusion), kind=kLoop, calls=%fused_computation.2 | loop fusion | flops 245760 | bytes 663712 | tf_op jit(solution)/shard_map/convert_element_type | solution.py:293
  1.8 0.0 copy-done.2
  1.8 0.0 copy-start
  1.8 0.0 copy-start.1
  1.8 0.2 bitcast_multiply_fusion.masked_ref
  2.0 0.6 %copy-done = f32[2,80,80]{2,1,0:T(8,128)S(1)} copy-done((f32[2,80,80]{2,1,0:T(8,128)S(1)}, f32[2,80,80]{2,1,0:T(8,128)}, u32[]{:S(2)}) %copy-start) | copy-done | bytes 51224
  2.7 0.0 copy-done.1
  2.7 34.3 %shard_map.55 = f32[2,5,16,8,128]{4,3,2,1,0:T(8,128)S(1)} custom-call(f32[2,16,40,128]{3,2,1,0:T(8,128)S(1)} %bitcast_multiply_fusion.masked_ref, f32[16,40,128]{2,1,0:T(8,128)S(1)} %fusion.wet_ref, f32[2,80,80]{2,1,0:T(8,128)S(1)} %copy-done, f32[2,16,128]{2,1,0:T(8,128)S(1)} %copy-done.1), custom_call_target="tpu_custom_call" | custom-call | flops 60000000 | bytes 4000000 | tf_op jit(solution)/shard_map/pallas_call | solution.py:298
  37.0 1.0 %copy.10 = f32[2,5,8,16,128]{4,3,2,1,0:T(8,128)} copy(f32[2,5,8,16,128]{4,2,3,1,0:T(8,128)S(1)} %bitcast.10) | data formatting | bytes 1310720 | tf_op jit(solution)/shard_map/transpose | solution.py:324
  (1 shorter events, 0.0 us)
Async XLA Ops:
  0.0 0.7 %copy-start.3 = (s32[16,128]{1,0:T(8,128)S(1)}, s32[16,128]{1,0:T(8,128)}, u32[]{:S(2)}) copy-start(s32[16,128]{1,0:T(8,128)} %param.9) | copy-start | bytes 24580
  0.0 1.8 %copy-start.2 = (f32[1,2,40,16,128]{4,3,2,1,0:T(8,128)S(1)}, f32[1,2,40,16,128]{4,3,2,1,0:T(8,128)}, u32[]{:S(2)}) copy-start(f32[1,2,40,16,128]{4,3,2,1,0:T(8,128)} %param.5) | copy-start | bytes 1966084
  1.8 0.9 %copy-start = (f32[2,80,80]{2,1,0:T(8,128)S(1)}, f32[2,80,80]{2,1,0:T(8,128)}, u32[]{:S(2)}) copy-start(f32[2,80,80]{2,1,0:T(8,128)} %corr_ref.1) | copy-start | bytes 153604
  1.8 0.9 %copy-start.1 = (f32[2,16,128]{2,1,0:T(8,128)S(1)}, f32[2,16,128]{2,1,0:T(8,128)}, u32[]{:S(2)}) copy-start(f32[2,16,128]{2,1,0:T(8,128)} %kappa_ref.1) | copy-start | bytes 49156
where the time goes:
time: 38.1 us; the launch traced here: 37.9 us
  Pallas kernels  34.3 us (90%)
  local copies, waits for them, and re-layouts  2.3 us (6%)
  other arithmetic  1.3 us (3%)
    pallas_call x1, Pallas kernels, fused(): pl.pallas_call(kernel, out_shape=jax.ShapeDtypeStruct((2, tiles, cells, T...  34.3 us
    unnamed x8, local copies, waits for them, and re-layouts  1.35 us
    convert_element_type x1, other arithmetic, fused(): (turned * (numbers[None, :, None] < level_count[:, None, :]).astype(jnp.i...  1.08 us
    transpose x1, local copies, waits for them, and re-layouts, fused(): return result.transpose(0, 1, 3, 2, 4).reshape(increments.shape)  0.95 us

commit v1 on v0

--- a/solution.py
+++ b/solution.py
@@ -102,9 +102,10 @@
 
 
 def kernel(
-    masked_ref, wet_ref, corr_ref, kappa_ref, out_ref,
+    inc_hbm, corr_hbm, kappa_hbm, sea_hbm, count_hbm, out_ref,
+    inc_ref, corr_ref, kappa_ref, sea_ref, count_ref, masked_ref,
     geo, own, other, field, halo, east, north, south,
-    own_sems, same_sems, cross_sems, geo_sems, halo_sems, out_sems,
+    own_sems, same_sems, cross_sems, geo_sems, halo_sems, out_sems, in_sems, keep_sems,
 ):
     lev, gx, gy = lax.axis_index("lev"), lax.axis_index("gx"), lax.axis_index("gy")
     count = lax.axis_size("gx")
@@ -121,14 +122,29 @@
     pair = {"lev": 1 - lev}
     cross = {"lev": 1 - lev, "gy": 1 - gy}
 
+    loads = [
+        pltpu.make_async_copy(src, dst, in_sems.at[n])
+        for n, (src, dst) in enumerate((
+            (sea_hbm, sea_ref), (count_hbm, count_ref), (kappa_hbm, kappa_ref),
+            (inc_hbm, inc_ref), (corr_hbm, corr_ref)))
+    ]
+    for load in loads:
+        load.start()
     barrier = pltpu.get_barrier_semaphore()
     everyone = (east_dev, west_dev, mate, pair, cross)
     for device in everyone:
         pl.semaphore_signal(barrier, inc=1, device_id=device, device_id_type=MESH)
     columns = gy * lanes + lax.broadcasted_iota(jnp.int32, (1, lanes), 1)
     is_open = (columns != lanes * lax.axis_size("gy") - 1).astype(jnp.float32)
-    geo[gy, width:width + cells, 0:levels] = wet_ref[...]
+    for load in loads:
+        load.wait()
+    number = lev * levels + lax.broadcasted_iota(jnp.int32, (levels, lanes), 0)
     for x in range(cells):
+        sea = sea_ref[pl.ds(x, levels, stride=cells), :]
+        value = jnp.where(number < count_ref[x:x + 1, :], sea, 0).astype(jnp.float32)
+        geo[gy, width + x, 0:levels] = value
+        for t in range(2):
+            masked_ref[t, x] = inc_ref[t, pl.ds(x, levels, stride=cells), :] * value
         geo[gy, width + x, levels:levels + 1] = kappa_ref[0, x:x + 1]
         geo[gy, width + x, levels + 1:levels + 2] = kappa_ref[1, x:x + 1] * is_open
         geo[gy, width + x, levels + 2:] = jnp.zeros((TILE - 2, lanes), jnp.float32)
@@ -275,7 +291,9 @@
                     field.at[k, pl.ds(width, cells), 1 - gy], out_ref.at[gy, k],
                     out_sems.at[0, k], out_sems.at[1, k], mate))
                 out_copies[-1].start()
-                out_ref[gy, k] = field[k, width:width + cells, gy]
+                out_copies.append(pltpu.make_async_copy(
+                    field.at[k, pl.ds(width, cells), gy], out_ref.at[gy, k], keep_sems.at[k]))
+                out_copies[-1].start()
         pending = later
     for copy in out_copies:
         copy.wait()
@@ -287,20 +305,21 @@
     width = WIDTH
     rows = cells + 2 * width
     rounds = PASSES // width
-    lev = lax.axis_index("lev")
-    numbers = lev * levels + jnp.arange(levels, dtype=jnp.int32)
-    turned = jnp.swapaxes(sea_mask, 0, 1)
-    wet = (turned * (numbers[None, :, None] < level_count[:, None, :]).astype(jnp.int32)).astype(jnp.float32)
-    masked = jnp.swapaxes(increments[0], 1, 2) * wet[None]
-    vmem = pl.BlockSpec(memory_space=pltpu.VMEM)
+    hbm = pl.BlockSpec(memory_space=pl.ANY)
     f32 = jnp.float32
     dma = pltpu.SemaphoreType.DMA
     result = pl.pallas_call(
         kernel,
         out_shape=jax.ShapeDtypeStruct((2, tiles, cells, TILE, lanes), f32),
-        in_specs=[vmem] * 4,
-        out_specs=vmem,
+        in_specs=[hbm] * 5,
+        out_specs=hbm,
         scratch_shapes=[
+            pltpu.VMEM((2, levels * cells, lanes), f32),
+            pltpu.VMEM(vert_corr.shape, f32),
+            pltpu.VMEM(kappa.shape, f32),
+            pltpu.VMEM((levels * cells, lanes), sea_mask.dtype),
+            pltpu.VMEM(level_count.shape, level_count.dtype),
+            pltpu.VMEM((2, cells, levels, lanes), f32),
             pltpu.VMEM((2, rows, levels + TILE, lanes), f32),
             pltpu.VMEM((cells, levels, lanes), f32),
             pltpu.VMEM((2, cells, levels, lanes), f32),
@@ -315,12 +334,17 @@
             dma((2, 5)),
             dma((2, rounds, 2, tiles)),
             dma((2, tiles)),
+            dma((5,)),
+            dma((tiles,)),
         ],
         compiler_params=pltpu.CompilerParams(
-            collective_id=0, has_side_effects=True, vmem_limit_bytes=32 * 1024 * 1024
+            collective_id=0, has_side_effects=True, vmem_limit_bytes=58 * 1024 * 1024
         ),
         cost_estimate=pl.CostEstimate(flops=60_000_000, bytes_accessed=4_000_000, transcendentals=0),
-    )(masked, wet, vert_corr, kappa)
+    )(
+        increments.reshape(2, levels * cells, lanes), vert_corr, kappa,
+        sea_mask.reshape(levels * cells, lanes), level_count,
+    )
     return result.transpose(0, 1, 3, 2, 4).reshape(increments.shape)
 
 

time: 38.1 us -> 37.1 us (0.974)
  other arithmetic: 1.3 us -> 0 us
  Pallas kernels: 34.3 us -> 34.9 us
    unnamed x8 -> x0, local copies, waits for them, and re-layouts: 1.35 us -> none
    transpose x1, local copies, waits for them, and re-layouts: 0.95 us -> 2.04 us  [fused(): return result.transpose(0, 1, 3, 2, 4).reshape(increments.shape)]
    convert_element_type x1 -> x0, other arithmetic: 1.08 us -> none  [fused(): (turned * (numbers[None, :, None] < level_count[:, None, :]).astype(jnp.i...]
    pallas_call x1, Pallas kernels: 34.3 us -> 34.9 us  [fused(): pl.pallas_call(kernel, out_shape=jax.ShapeDtypeStruct((2, tiles, cells, T...]
where the time goes in v1:
time: 37.1 us; the launch traced here: 37 us
  Pallas kernels  34.9 us (94%)
  local copies, waits for them, and re-layouts  2.04 us (5%)
    pallas_call x1, Pallas kernels, fused(): pl.pallas_call(kernel, out_shape=jax.ShapeDtypeStruct((2, tiles, cells, T...  34.9 us
    transpose x1, local copies, waits for them, and re-layouts, fused(): return result.transpose(0, 1, 3, 2, 4).reshape(increments.shape)  2.04 us

profile of v1, /device:TPU:0, one launch (start us, length us, event | category | flops | bytes accessed | tf_op | source)
XLA Modules:
  0.0 37.0 jit_solution(12828287912739701846)
XLA Ops:
  0.0 34.9 %shard_map.55 = f32[2,5,16,8,128]{4,3,2,1,0:T(8,128)} custom-call(f32[2,640,128]{2,1,0:T(8,128)} %bitcast.5, f32[2,80,80]{2,1,0:T(8,128)} %corr_hbm.1, f32[2,16,128]{2,1,0:T(8,128)} %kappa_hbm.1, s32[640,128]{1,0:T(8,128)} %bitcast.6, s32[16,128]{1,0:T(8,128)} %count_hbm.1), custom_call_target="tpu_custom_call" | custom-call | flops 60000000 | bytes 4000000 | tf_op jit(solution)/shard_map/pallas_call | solution.py:311
  34.9 2.0 %copy.6 = f32[2,5,8,16,128]{4,3,2,1,0:T(8,128)} copy(f32[2,5,8,16,128]{4,2,3,1,0:T(8,128)} %bitcast.4) | data formatting | bytes 1310720 | tf_op jit(solution)/shard_map/transpose | solution.py:348

commit v2 on v1

--- a/solution.py
+++ b/solution.py
@@ -104,7 +104,7 @@
 def kernel(
     inc_hbm, corr_hbm, kappa_hbm, sea_hbm, count_hbm, out_ref,
     inc_ref, corr_ref, kappa_ref, sea_ref, count_ref, masked_ref,
-    geo, own, other, field, halo, east, north, south,
+    geo, own, other, field, halo, east, north, south, stage,
     own_sems, same_sems, cross_sems, geo_sems, halo_sems, out_sems, in_sems, keep_sems,
 ):
     lev, gx, gy = lax.axis_index("lev"), lax.axis_index("gx"), lax.axis_index("gy")
@@ -174,11 +174,10 @@
     for q in range(len(starts)):
         same_copies[q].start()
         cross_copies[q].start()
+        own_copies[q].start()
         if q == 0:
-            for copy in geo_copies[1:]:
+            for copy in geo_copies:
                 copy.start()
-            geo_copies[0].start()
-        own_copies[q].start()
 
     mine = corr_ref[gy, pl.ds(pl.multiple_of(lev * levels, TILE), levels), :]
     swapped = jnp.concatenate([mine[:, levels:], mine[:, :levels]], axis=1)
@@ -272,7 +271,10 @@
                 for h in range(2):
                     wet = geo[h, row, k * TILE:(k + 1) * TILE]
                     total = here[h] + ((ahead[h] - flux[h]) + (rise[h] - down[h]))
-                    field[k, row, h] = wet * total
+                    if r == rounds - 1 and step == width - 1:
+                        stage[k, h, pl.ds(row - width, TILE, stride=cells), :] = wet * total
+                    else:
+                        field[k, row, h] = wet * total
                 here, flux = after, ahead
 
     out_copies = []
@@ -288,11 +290,11 @@
                     copy.start()
             else:
                 out_copies.append(remote(
-                    field.at[k, pl.ds(width, cells), 1 - gy], out_ref.at[gy, k],
+                    stage.at[k, 1 - gy], out_ref.at[gy, k],
                     out_sems.at[0, k], out_sems.at[1, k], mate))
                 out_copies[-1].start()
                 out_copies.append(pltpu.make_async_copy(
-                    field.at[k, pl.ds(width, cells), gy], out_ref.at[gy, k], keep_sems.at[k]))
+                    stage.at[k, gy], out_ref.at[gy, k], keep_sems.at[k]))
                 out_copies[-1].start()
         pending = later
     for copy in out_copies:
@@ -310,9 +312,9 @@
     dma = pltpu.SemaphoreType.DMA
     result = pl.pallas_call(
         kernel,
-        out_shape=jax.ShapeDtypeStruct((2, tiles, cells, TILE, lanes), f32),
+        out_shape=jax.ShapeDtypeStruct((2, tiles, TILE * cells, lanes), f32),
         in_specs=[hbm] * 5,
-        out_specs=hbm,
+        out_specs=pl.BlockSpec(memory_space=pltpu.VMEM),
         scratch_shapes=[
             pltpu.VMEM((2, levels * cells, lanes), f32),
             pltpu.VMEM(vert_corr.shape, f32),
@@ -328,6 +330,7 @@
             pltpu.VMEM((rows, 2, TILE, lanes), f32),
             pltpu.VMEM((rows, 2, TILE, lanes), f32),
             pltpu.VMEM((rows, 2, TILE, lanes), f32),
+            pltpu.VMEM((tiles, 2, TILE * cells, lanes), f32),
             dma((2, 3)),
             dma((2, 3)),
             dma((2, 3)),
@@ -338,14 +341,15 @@
             dma((tiles,)),
         ],
         compiler_params=pltpu.CompilerParams(
-            collective_id=0, has_side_effects=True, vmem_limit_bytes=58 * 1024 * 1024
+            collective_id=0, has_side_effects=True, vmem_limit_bytes=32 * 1024 * 1024
         ),
         cost_estimate=pl.CostEstimate(flops=60_000_000, bytes_accessed=4_000_000, transcendentals=0),
     )(
-        increments.reshape(2, levels * cells, lanes), vert_corr, kappa,
-        sea_mask.reshape(levels * cells, lanes), level_count,
-    )
-    return result.transpose(0, 1, 3, 2, 4).reshape(increments.shape)
+        *(pltpu.with_memory_space_constraint(v, pltpu.HBM) for v in (
+            increments.reshape(2, levels * cells, lanes), vert_corr, kappa,
+            sea_mask.reshape(levels * cells, lanes), level_count))
+    )
+    return result.reshape(increments.shape)
 
 
 def fits(mesh):

time: 37.1 us -> 35.8 us (0.965)
  local copies, waits for them, and re-layouts: 2.04 us -> 0.84 us
    transpose x1 -> x0, local copies, waits for them, and re-layouts: 2.04 us -> none  [fused(): return result.transpose(0, 1, 3, 2, 4).reshape(increments.shape)]
    unnamed x0 -> x1, local copies, waits for them, and re-layouts: none -> 0.84 us
where the time goes in v2:
time: 35.8 us; the launch traced here: 35.6 us
  Pallas kernels  34.8 us (97%)
  local copies, waits for them, and re-layouts  0.84 us (2%)
    pallas_call x1, Pallas kernels, fused(): pl.pallas_call(kernel, out_shape=jax.ShapeDtypeStruct((2, tiles, TILE * c...  34.8 us
    unnamed x1, local copies, waits for them, and re-layouts  0.84 us

profile of v2, /device:TPU:0, one launch (start us, length us, event | category | flops | bytes accessed | tf_op | source)
XLA Modules:
  0.0 35.6 jit_solution(8842108682830570854)
XLA Ops:
  0.0 34.8 %shard_map.55 = f32[2,5,128,128]{3,2,1,0:T(8,128)S(1)} custom-call(f32[2,640,128]{2,1,0:T(8,128)} %bitcast.4, f32[2,80,80]{2,1,0:T(8,128)} %corr_hbm.1, f32[2,16,128]{2,1,0:T(8,128)} %kappa_hbm.1, s32[640,128]{1,0:T(8,128)} %bitcast.5, s32[16,128]{1,0:T(8,128)} %count_hbm.1), custom_call_target="tpu_custom_call" | custom-call | flops 60000000 | bytes 4000000 | tf_op jit(solution)/shard_map/pallas_call | solution.py:313
  34.8 0.8 %copy.7 = f32[1,2,40,16,128]{4,3,2,1,0:T(8,128)} copy(f32[1,2,40,16,128]{4,3,2,1,0:T(8,128)S(1)} %bitcast.3) | data formatting | bytes 1310720

commit v3 on v2

--- a/solution.py
+++ b/solution.py
@@ -150,7 +150,9 @@
         geo[gy, width + x, levels + 2:] = jnp.zeros((TILE - 2, lanes), jnp.float32)
     pl.semaphore_wait(barrier, len(everyone))
 
-    starts = ((0, width), (cells - width, width), (width, cells - 2 * width))
+    middle = (cells - 2 * width) // 2
+    starts = (
+        (0, width), (cells - width, width), (width, middle), (width + middle, cells - 2 * width - middle))
     own_copies, same_copies, cross_copies = [], [], []
     for q, (start, size) in enumerate(starts):
         span = pl.ds(start, size)
@@ -171,13 +173,13 @@
                geo.at[gy, pl.ds(width + cells, width)],
                geo_sems.at[0, 2], geo_sems.at[1, 2], west_dev),
     ]
+    for copy in geo_copies[1:]:
+        copy.start()
+    geo_copies[0].start()
     for q in range(len(starts)):
         same_copies[q].start()
         cross_copies[q].start()
         own_copies[q].start()
-        if q == 0:
-            for copy in geo_copies:
-                copy.start()
 
     mine = corr_ref[gy, pl.ds(pl.multiple_of(lev * levels, TILE), levels), :]
     swapped = jnp.concatenate([mine[:, levels:], mine[:, :levels]], axis=1)
@@ -331,9 +333,9 @@
             pltpu.VMEM((rows, 2, TILE, lanes), f32),
             pltpu.VMEM((rows, 2, TILE, lanes), f32),
             pltpu.VMEM((tiles, 2, TILE * cells, lanes), f32),
-            dma((2, 3)),
-            dma((2, 3)),
-            dma((2, 3)),
+            dma((2, 4)),
+            dma((2, 4)),
+            dma((2, 4)),
             dma((2, 5)),
             dma((2, rounds, 2, tiles)),
             dma((2, tiles)),

time: 35.8 us -> 35.8 us (level)
  no operation moved by 1% of the time
where the time goes in v3:
time: 35.8 us; the launch traced here: 35.7 us
  Pallas kernels  34.8 us (97%)
  local copies, waits for them, and re-layouts  0.84 us (2%)
    pallas_call x1, Pallas kernels, fused(): pl.pallas_call(kernel, out_shape=jax.ShapeDtypeStruct((2, tiles, TILE * c...  34.8 us
    unnamed x1, local copies, waits for them, and re-layouts  0.84 us

profile of v3, /device:TPU:0, one launch (start us, length us, event | category | flops | bytes accessed | tf_op | source)
XLA Modules:
  0.0 35.7 jit_solution(9166142584999472511)
XLA Ops:
  0.0 34.8 %shard_map.55 = f32[2,5,128,128]{3,2,1,0:T(8,128)S(1)} custom-call(f32[2,640,128]{2,1,0:T(8,128)} %bitcast.4, f32[2,80,80]{2,1,0:T(8,128)} %corr_hbm.1, f32[2,16,128]{2,1,0:T(8,128)} %kappa_hbm.1, s32[640,128]{1,0:T(8,128)} %bitcast.5, s32[16,128]{1,0:T(8,128)} %count_hbm.1), custom_call_target="tpu_custom_call" | custom-call | flops 60000000 | bytes 4000000 | tf_op jit(solution)/shard_map/pallas_call | solution.py:315
  34.8 0.8 %copy.7 = f32[1,2,40,16,128]{4,3,2,1,0:T(8,128)} copy(f32[1,2,40,16,128]{4,3,2,1,0:T(8,128)S(1)} %bitcast.3) | data formatting | bytes 1310720
